TPU v7x, 32 devices: a whole 2x2x4 slice. The times are simulated.
32 devices in a mesh: blk: 4 (over y, x), grp: 8 (over z, core).
Axes of the slice: x: 2, y: 2, z: 4, core: 2. Of those that a mesh axis runs over, the one named last changes fastest.
Arguments:
- field: float32 [128, 192, 512], P('grp', 'blk'), may hold values from -7 to 7
- x_panel: float32 [192, 144], P('blk'), as said below
- y_factor: float32 [128, 128], replicated, as said below
- z_factor: float32 [512, 512], replicated, as said below
- scaling: float32 [128, 192, 512], P('grp', 'blk'), may hold values from 0.3 to 3
Outputs:
- updated: float32 [128, 192, 512], P('grp', 'blk')
Inputs may be any that keep to these rules, and one draw needn't show every extreme that they name: x_panel[x, j] is zero where j - 48 - (x mod 48) lies outside -48 to 48. y_factor[i, k] is zero where the periodic distance of i and k exceeds 48. z_factor[i, k] is zero where the periodic distance of i and k exceeds 48.
All inputs are finite; a program needn't handle non-finite values.
Results may differ from a plain program's by a relative error of at most 0.0003.
Values sent between devices are 32-bit elements; how exact they have to be, the bound alone decides.
A program may use at most 64 MiB of HBM per device.

v0:
```python
import jax
import jax.numpy as jnp
from jax import lax
from jax.sharding import PartitionSpec as P

HOR = 48


def padded(cells, sides, width):
    for axis, dim in sides:
        count = lax.axis_size(axis)
        head = lax.slice_in_dim(cells, 0, width, axis=dim)
        tail = lax.slice_in_dim(cells, cells.shape[dim] - width, cells.shape[dim], axis=dim)
        cells = jnp.concatenate(
            [
                lax.ppermute(tail, axis, [(i, (i + 1) % count) for i in range(count)]),
                cells,
                lax.ppermute(head, axis, [((i + 1) % count, i) for i in range(count)]),
            ],
            axis=dim,
        )
    return cells


def apply_depth(block, z_factor):
    return lax.dot_general(
        block, z_factor, (((2,), (1,)), ((), ())), precision=lax.Precision.HIGHEST
    )


def apply_planes(x_panel, widened):
    return jnp.einsum("rj,yjz->yrz", x_panel, widened, precision=lax.Precision.HIGHEST)


def apply_across(block, y_factor):
    rows_here, planes, cells = block.shape
    flat = block.reshape(rows_here, planes * cells)
    pencils = lax.all_to_all(flat, "grp", split_axis=1, concat_axis=0, tiled=True)
    turned = jnp.dot(y_factor, pencils, precision=lax.Precision.HIGHEST)
    back = lax.all_to_all(turned, "grp", split_axis=0, concat_axis=1, tiled=True)
    return back.reshape(rows_here, planes, cells)


def on_device(field, x_panel, y_factor, z_factor, scaling):
    widened = padded(field, (("blk", 1),), HOR)
    planes_done = apply_planes(x_panel, widened)
    depth = apply_depth(planes_done, z_factor)
    along = apply_across(depth, y_factor)
    return along * scaling


def solution(mesh):
    in_specs = (P("grp", "blk", None), P("blk", None), P(), P(), P("grp", "blk", None))
    out_specs = P("grp", "blk", None)
    return jax.shard_map(
        on_device, mesh=mesh, in_specs=in_specs, out_specs=out_specs, check_vma=False
    )
```

profile of v0, /device:TPU:0, one launch (start us, length us, event | category | flops | bytes accessed | tf_op | source)
XLA Modules:
  0.0 173.6 jit_solution(6990499878261344672)
XLA Ops:
  0.0 0.0 copy-start
  0.0 2.9 %collective-permute-start = (f32[16,48,512]{2,1,0:T(8,128)}, f32[16,48,512]{2,1,0:T(8,128)S(1)}, u32[]{:S(2)}, u32[]{:S(2)}) collective-permute-start(f32[16,48,512]{2,1,0:T(8,128)} %param.5), channel_id=1, source_target_pairs={{0,8},{8,16},{16,24},{24,0},{1,9},{9,17},{17,25},{25,1},{2,10},{10... | collective-permute-start | bytes 4718600 | tf_op jit(solution)/shard_map/ppermute | solution.py:16
  2.9 1.0 collective-permute-start.1
  4.0 35.4 %collective-permute-done = f32[16,48,512]{2,1,0:T(8,128)S(1)} collective-permute-done((f32[16,48,512]{2,1,0:T(8,128)}, f32[16,48,512]{2,1,0:T(8,128)S(1)}, u32[]{:S(2)}, u32[]{:S(2)}) %collective-permute-start) | collective-permute-done | bytes 1572896 | tf_op jit(solution)/shard_map/ppermute | solution.py:16
  39.3 33.1 %collective-permute-done.1 = f32[16,48,512]{2,1,0:T(8,128)S(1)} collective-permute-done((f32[16,48,512]{2,1,0:T(8,128)}, f32[16,48,512]{2,1,0:T(8,128)S(1)}, u32[]{:S(2)}, u32[]{:S(2)}) %collective-permute-start.1) | collective-permute-done | bytes 1572896 | tf_op jit(solution)/shard_map/ppermute | solution.py:18
  72.5 4.1 %fusion = f32[16,512,48]{1,2,0:T(8,128)S(1)} fusion(f32[16,48,512]{2,1,0:T(8,128)S(1)} %collective-permute-done.1, f32[16,48,512]{2,1,0:T(8,128)} %param.5, f32[16,48,512]{2,1,0:T(8,128)S(1)} %collective-permute-done, f32[48,144]{1,0:T(8,128)} %param.6), kind=kOutput, calls=%fused_computation | convolution fusion | flops 681836544 | bytes 6319104 | tf_op jit(solution)/shard_map/rj,yjz->yrz/dot_general | solution.py:32
  76.6 0.0 copy-done
  76.6 3.8 %fusion.6 = f32[16,48,512]{2,1,0:T(8,128)} fusion(f32[16,512,48]{1,2,0:T(8,128)S(1)} %fusion, f32[512,512]{1,0:T(8,128)S(1)} %copy-done), kind=kOutput, calls=%fused_computation.6 | convolution fusion | flops 2415919104 | bytes 4194304 | tf_op jit(solution)/shard_map/dot_general | solution.py:26
  80.4 2.0 %all_to_all.26 = f32[16,8,3072]{2,1,0:T(8,128)S(1)} reshape(f32[16,48,512]{2,1,0:T(8,128)} %fusion.6) | data formatting | bytes 3145728 | tf_op jit(solution)/shard_map/all_to_all | solution.py:38
  82.4 0.9 copy.7
  83.4 0.0 copy-start.1
  83.4 42.6 %all_to_all.35 = f32[16,8,3072]{2,0,1:T(8,128)S(1)} all-to-all(f32[16,8,3072]{2,0,1:T(8,128)S(1)} %copy.7), channel_id=1, replica_groups=mesh['blk'=4,'grp'=8] {'grp'}, dimensions={1} | all-to-all | bytes 3145728 | tf_op jit(solution)/shard_map/all_to_all | solution.py:38
  126.0 0.0 copy-done.1
  126.0 1.5 fusion.11
  127.5 40.3 %all_to_all.36 = f32[8,16,3072]{2,1,0:T(8,128)S(1)} all-to-all(f32[8,16,3072]{2,1,0:T(8,128)S(1)} %bitcast.19), channel_id=1, replica_groups=mesh['blk'=4,'grp'=8] {'grp'}, dimensions={0} | all-to-all | bytes 3145728 | tf_op jit(solution)/shard_map/all_to_all | solution.py:40
  167.8 0.9 copy.8
  168.7 1.5 reshape.12
  170.2 3.4 %mul.3 = f32[16,48,512]{2,1,0:T(8,128)} multiply(f32[16,48,512]{2,1,0:T(8,128)} %reshape.12, f32[16,48,512]{2,1,0:T(8,128)} %param.9) | non-fusion elementwise | flops 393216 | bytes 4718592 | tf_op jit(solution)/shard_map/mul | solution.py:49
Async XLA Ops:
  0.0 76.6 %copy-start = (f32[512,512]{1,0:T(8,128)S(1)}, f32[512,512]{1,0:T(8,128)}, u32[]{:S(2)}) copy-start(f32[512,512]{1,0:T(8,128)} %param.8) | copy-start | bytes 3145732
  0.0 39.3 %collective-permute-start = (f32[16,48,512]{2,1,0:T(8,128)}, f32[16,48,512]{2,1,0:T(8,128)S(1)}, u32[]{:S(2)}, u32[]{:S(2)}) collective-permute-start(f32[16,48,512]{2,1,0:T(8,128)} %param.5), channel_id=1, source_target_pairs={{0,8},{8,16},{16,24},{24,0},{1,9},{9,17},{17,25},{25,1},{2,10},{10... | collective-permute-start | bytes 4718600 | tf_op jit(solution)/shard_map/ppermute | solution.py:16
  2.9 69.5 %collective-permute-start.1 = (f32[16,48,512]{2,1,0:T(8,128)}, f32[16,48,512]{2,1,0:T(8,128)S(1)}, u32[]{:S(2)}, u32[]{:S(2)}) collective-permute-start(f32[16,48,512]{2,1,0:T(8,128)} %param.5), channel_id=1, source_target_pairs={{8,0},{16,8},{24,16},{0,24},{9,1},{17,9},{25,17},{1,25},{10,2},{18... | collective-permute-start | bytes 4718600 | tf_op jit(solution)/shard_map/ppermute | solution.py:18
  83.4 42.7 %copy-start.1 = (f32[128,128]{1,0:T(8,128)S(1)}, f32[128,128]{1,0:T(8,128)}, u32[]{:S(2)}) copy-start(f32[128,128]{1,0:T(8,128)} %param.7) | copy-start | bytes 196612
where the time goes:
time: 174 us
  blocking collectives  82.9 us (48%)
  waiting for transfers between devices  68.5 us (39%)
  matrix products  9.48 us (5%)
  local copies, waits for them, and re-layouts  5.3 us (3%)
  starting transfers between devices  3.95 us (2%)
  other arithmetic  3.42 us (2%)
    all_to_all x1, blocking collectives, apply_across(): lax.all_to_all(flat, 'grp', split_axis=1, concat_axis=0, tiled=True)  42.6 us
    all_to_all x1, blocking collectives, apply_across(): lax.all_to_all(turned, 'grp', split_axis=0, concat_axis=1, tiled=True)  40.3 us
    ppermute x1, waiting for transfers between devices, padded(): lax.ppermute(tail, axis, [(i, (i + 1) % count) for i in range(count)])  35.4 us
    ppermute x1, waiting for transfers between devices, padded(): lax.ppermute(head, axis, [((i + 1) % count, i) for i in range(count)])  33.1 us
    dot_general x1, matrix products, apply_planes(): jnp.einsum('rj,yjz->yrz', x_panel, widened, precision=lax.Precision.HIGHEST)  4.14 us
    dot_general x1, matrix products, apply_depth(): lax.dot_general(block, z_factor, (((2,), (1,)), ((), ())), precision=lax....  3.82 us
  transfers between devices with their start and end apart: 2, of which 2 were waited for; matrix products, arithmetic and copies ran while one was open for 0% of the time, Pallas kernels for 0%

commit v1 on v0

--- a/solution.py
+++ b/solution.py
@@ -1,9 +1,17 @@
+import functools
+
 import jax
 import jax.numpy as jnp
 from jax import lax
+from jax.experimental import pallas as pl
+from jax.experimental.pallas import tpu as pltpu
 from jax.sharding import PartitionSpec as P
 
-HOR = 48
+LANES = 128
+SUB = 16
+MESH = pl.DeviceIdType.MESH
+F32 = jnp.float32
+BF16 = jnp.bfloat16
 
 
 def padded(cells, sides, width):
@@ -41,12 +49,263 @@
     return back.reshape(rows_here, planes, cells)
 
 
-def on_device(field, x_panel, y_factor, z_factor, scaling):
-    widened = padded(field, (("blk", 1),), HOR)
+def plain(field, x_panel, y_factor, z_factor, scaling):
+    width = (x_panel.shape[1] - field.shape[1]) // 2
+    widened = padded(field, (("blk", 1),), width)
     planes_done = apply_planes(x_panel, widened)
     depth = apply_depth(planes_done, z_factor)
     along = apply_across(depth, y_factor)
     return along * scaling
+
+
+def split(value):
+    high = value.astype(BF16)
+    return high, (value - high.astype(F32)).astype(BF16)
+
+
+def stacked(value):
+    high, low = split(value)
+    return jnp.concatenate([high, low], axis=0), high
+
+
+def times(both, high, right):
+    right_high, right_low = split(right)
+    rows = high.shape[0]
+    first = jnp.dot(both, right_high, preferred_element_type=F32)
+    second = jnp.dot(high, right_low, preferred_element_type=F32)
+    return first[:rows] + (first[rows:] + second)
+
+
+def kernel(
+    n_grp, n_blk, field, panel, y_factor, z_factor, scaling, out,
+    field_high, field_low, own, partner, other, turned, gathered, mixed, back,
+    f_send, f_recv, b_send, b_recv, h1_send, h1_recv, h2_send, h2_recv,
+):
+    rows, planes, cells = field.shape
+    chunks = cells // LANES
+    share = planes // n_grp
+    piece = share * rows
+    parts = h1_send.shape[1]
+    part_rows = rows // parts
+    grp = lax.axis_index("grp")
+    blk = lax.axis_index("blk")
+    even = lax.rem(blk, 2) == 0
+    mate = jnp.where(even, blk + 1, blk - 1)
+    ahead = lax.rem(jnp.where(even, blk + 2, blk + n_blk - 2), n_blk)
+    behind = lax.rem(jnp.where(even, blk + n_blk - 2, blk + 2), n_blk)
+
+    offsets = sorted(range(1, n_grp), key=lambda s: (-min(s, n_grp - s), s))
+    barrier = pltpu.get_barrier_semaphore()
+    for step in offsets:
+        pl.semaphore_signal(
+            barrier, inc=1, device_id={"grp": lax.rem(grp + step, n_grp)}, device_id_type=MESH
+        )
+    pl.semaphore_signal(barrier, inc=1, device_id={"blk": mate}, device_id_type=MESH)
+    pl.semaphore_signal(barrier, inc=1, device_id={"blk": behind}, device_id_type=MESH)
+
+    def depth(chunk):
+        z_both, z_high = stacked(z_factor[chunk * LANES:(chunk + 1) * LANES, :])
+        turn = (((1,), (1,)), ((), ()))
+        for y in range(0, rows, part_rows // 2):
+            y_end = y + part_rows // 2
+            here = slice(y * planes, y_end * planes)
+            first = lax.dot_general(field_high[here, :], z_both, turn, preferred_element_type=F32)
+            second = lax.dot_general(field_low[here, :], z_high, turn, preferred_element_type=F32)
+            result = first[:, :LANES] + (first[:, LANES:] + second)
+            own[chunk, y:y_end] = result.reshape(y_end - y, planes, LANES)
+
+    def rows_of(y):
+        return pl.ds(y, planes, stride=rows)
+
+    def scatter(chunk):
+        for step in offsets:
+            to = lax.rem(grp + step, n_grp)
+            pltpu.make_async_remote_copy(
+                src_ref=turned.at[chunk, pl.ds(pl.multiple_of(to * piece, SUB), piece)],
+                dst_ref=gathered.at[chunk, grp],
+                send_sem=f_send.at[chunk],
+                recv_sem=f_recv.at[chunk],
+                device_id={"grp": to},
+                device_id_type=MESH,
+            ).start()
+        gathered[chunk, grp] = turned[chunk, pl.ds(pl.multiple_of(grp * piece, SUB), piece), :]
+
+    def wait_for(ref, sem):
+        pltpu.make_async_copy(ref, ref, sem).wait()
+
+    def across(chunk):
+        wait_for(gathered.at[chunk, pl.ds(0, n_grp - 1)], f_recv.at[chunk])
+        y_both, y_high = stacked(y_factor[...])
+        for at in range(share):
+            pencils = jnp.concatenate(
+                [gathered[chunk, g, at * rows:(at + 1) * rows, :] for g in range(n_grp)], axis=0
+            )
+            result = times(y_both, y_high, pencils)
+            for g in range(n_grp):
+                mixed[chunk, g, at * rows:(at + 1) * rows, :] = result[g * rows:(g + 1) * rows]
+        for step in offsets:
+            to = lax.rem(grp + step, n_grp)
+            pltpu.make_async_remote_copy(
+                src_ref=mixed.at[chunk, to],
+                dst_ref=back.at[chunk, pl.ds(pl.multiple_of(grp * piece, SUB), piece)],
+                send_sem=b_send.at[chunk],
+                recv_sem=b_recv.at[chunk],
+                device_id={"grp": to},
+                device_id_type=MESH,
+            ).start()
+        back[chunk, pl.ds(pl.multiple_of(grp * piece, SUB), piece), :] = mixed[chunk, grp]
+
+    def wait_back(chunk):
+        wait_for(back.at[chunk, pl.ds(0, (n_grp - 1) * piece)], b_recv.at[chunk])
+
+    def part(chunk, at):
+        return (chunk, pl.ds(at * part_rows, part_rows))
+
+    def swap(chunk, at):
+        return pltpu.make_async_remote_copy(
+            src_ref=own.at[part(chunk, at)],
+            dst_ref=partner.at[part(chunk, at)],
+            send_sem=h1_send.at[chunk, at],
+            recv_sem=h1_recv.at[chunk, at],
+            device_id={"blk": mate},
+            device_id_type=MESH,
+        )
+
+    def forward(chunk, at):
+        return pltpu.make_async_remote_copy(
+            src_ref=partner.at[part(chunk, at)],
+            dst_ref=other.at[part(chunk, at)],
+            send_sem=h2_send.at[chunk, at],
+            recv_sem=h2_recv.at[chunk, at],
+            device_id={"blk": ahead},
+            device_id_type=MESH,
+        )
+
+    def pass_on(chunk):
+        for at in range(parts):
+            swap(chunk, at).wait_recv()
+            forward(chunk, at).start()
+
+    def along(chunk, store):
+        left, mid, right = (panel[:, i * planes:(i + 1) * planes] for i in range(3))
+        factor = jnp.concatenate(
+            [mid, jnp.where(even, right, left), jnp.where(even, left, right)], axis=1
+        )
+        x_both, x_high = stacked(factor)
+        for at in range(parts):
+            forward(chunk, at).wait_recv()
+            for y in range(at * part_rows, (at + 1) * part_rows, 2):
+                wide = jnp.concatenate(
+                    [
+                        jnp.concatenate([held[chunk, y + k] for held in (own, partner, other)], axis=0)
+                        for k in range(2)
+                    ],
+                    axis=1,
+                )
+                result = times(x_both, x_high, wide)
+                for k in range(2):
+                    store(chunk, y + k, result[:, k * LANES:(k + 1) * LANES])
+
+    def store_turned(chunk, y, value):
+        turned[chunk, rows_of(y), :] = value
+
+    def store_out(chunk, y, value):
+        lanes = slice(chunk * LANES, (chunk + 1) * LANES)
+        out[y, :, lanes] = value * scaling[y, :, lanes]
+
+    flat = field[...].reshape(rows * planes, cells)
+    field_high[...], field_low[...] = split(flat)
+    depth(0)
+    for y in range(rows):
+        store_turned(0, y, own[0, y])
+    pl.semaphore_wait(barrier, len(offsets) + 2)
+    scatter(0)
+    for chunk in range(1, chunks):
+        depth(chunk)
+        for at in range(parts):
+            swap(chunk, at).start()
+
+    def first_home():
+        wait_back(0)
+        for y in range(rows):
+            own[0, y] = back[0, rows_of(y), :]
+        for at in range(parts):
+            swap(0, at).start()
+
+    for chunk in range(1, chunks):
+        pass_on(chunk)
+        if chunk == 1:
+            across(0)
+        elif chunk == 2:
+            first_home()
+        else:
+            across(chunk - 2)
+        along(chunk, store_turned)
+        scatter(chunk)
+    if chunks < 2:
+        across(0)
+    if chunks < 3:
+        first_home()
+    pass_on(0)
+    late = range(max(1, chunks - 2), chunks)
+    for chunk in late[:-1]:
+        across(chunk)
+    along(0, store_out)
+    for chunk in late[-1:]:
+        across(chunk)
+    for chunk in range(1, chunks):
+        wait_back(chunk)
+        for y in range(rows):
+            store_out(chunk, y, back[chunk, rows_of(y), :])
+    for chunk in range(chunks):
+        wait_for(gathered.at[chunk, pl.ds(0, n_grp - 1)], f_send.at[chunk])
+        wait_for(gathered.at[chunk, pl.ds(0, n_grp - 1)], b_send.at[chunk])
+        for at in range(parts):
+            swap(chunk, at).wait_send()
+            forward(chunk, at).wait_send()
+
+
+def fused(field, x_panel, y_factor, z_factor, scaling):
+    n_grp, n_blk = lax.axis_size("grp"), lax.axis_size("blk")
+    rows, planes, cells = field.shape
+    chunks = cells // LANES
+    piece = planes // n_grp * rows
+    parts = 2
+    whole = pl.BlockSpec(memory_space=pltpu.VMEM)
+    held = pltpu.VMEM((chunks, rows, planes, LANES), F32)
+    turned = pltpu.VMEM((chunks, planes * rows, LANES), F32)
+    pieces = pltpu.VMEM((chunks, n_grp, piece, LANES), F32)
+    return pl.pallas_call(
+        functools.partial(kernel, n_grp, n_blk),
+        out_shape=jax.ShapeDtypeStruct(field.shape, F32),
+        in_specs=[whole] * 5,
+        out_specs=whole,
+        scratch_shapes=[pltpu.VMEM((rows * planes, cells), BF16)] * 2
+        + [held] * 3
+        + [turned, pieces, pieces, turned]
+        + [pltpu.SemaphoreType.DMA((chunks,))] * 4
+        + [pltpu.SemaphoreType.DMA((chunks, parts))] * 4,
+        compiler_params=pltpu.CompilerParams(
+            collective_id=0, has_side_effects=True, vmem_limit_bytes=48 * 2**20
+        ),
+    )(field, x_panel, y_factor, z_factor, scaling)
+
+
+def on_device(field, x_panel, y_factor, z_factor, scaling):
+    n_grp, n_blk = lax.axis_size("grp"), lax.axis_size("blk")
+    rows, planes, cells = field.shape
+    fits = (
+        x_panel.shape[1] == 3 * planes
+        and n_blk >= 4
+        and n_blk % 2 == 0
+        and n_grp >= 2
+        and planes % n_grp == 0
+        and planes % SUB == 0
+        and rows % SUB == 0
+        and cells % LANES == 0
+    )
+    step = fused if fits else plain
+    return step(field, x_panel, y_factor, z_factor, scaling)
 
 
 def solution(mesh):

time: 174 us -> 82.5 us (0.47)
  blocking collectives: 82.9 us -> 0 us
  Pallas kernels: 0 us -> 74.9 us
  waiting for transfers between devices: 68.5 us -> 0 us
  matrix products: 9.48 us -> 0 us
  starting transfers between devices: 3.95 us -> 0 us
  other arithmetic: 3.42 us -> 0 us
    all_to_all x2 -> x0, blocking collectives: 82.9 us -> none  [the longest x1 42.6 us: apply_across(): lax.all_to_all(flat, 'grp', split_axis=1, concat_axis=0, tiled=True)]
    pallas_call x0 -> x1, Pallas kernels: none -> 74.9 us  [fused(): pl.pallas_call(functools.partial(kernel, n_grp, n_blk), out_shape=jax.Sha...]
    ppermute x2 -> x0, waiting for transfers between devices: 68.5 us -> none  [the longest x1 35.4 us: padded(): lax.ppermute(tail, axis, [(i, (i + 1) % count) for i in range(count)])]
    dot_general x3 -> x0, matrix products: 9.48 us -> none  [the longest x1 4.14 us: apply_planes(): jnp.einsum('rj,yjz->yrz', x_panel, widened, precision=lax.Precision.HIGHEST)]
    unnamed x4 -> x11, local copies, waits for them, and re-layouts: 0.01 us -> 6.82 us
    ppermute x2 -> x0, starting transfers between devices: 3.95 us -> none  [the longest x1 2.94 us: padded(): lax.ppermute(tail, axis, [(i, (i + 1) % count) for i in range(count)])]
    all_to_all x3 -> x0, local copies, waits for them, and re-layouts: 3.82 us -> none  [the longest x2 2.91 us: apply_across(): lax.all_to_all(flat, 'grp', split_axis=1, concat_axis=0, tiled=True)]
    mul x1 -> x0, other arithmetic: 3.42 us -> none  [on_device(): return along * scaling]
  transfers between devices with their start and end apart: 2 -> 0, of which waited for: 2 -> 0; matrix products, arithmetic and copies ran while one was open for 0% -> 0% of each run, Pallas kernels for 0% -> 0%
where the time goes in v1:
time: 82.5 us; the launch traced here: 81.7 us
  Pallas kernels  74.9 us (91%)
  local copies, waits for them, and re-layouts  6.82 us (8%)
    pallas_call x1, Pallas kernels, fused(): pl.pallas_call(functools.partial(kernel, n_grp, n_blk), out_shape=jax.Sha...  74.9 us
    unnamed x11, local copies, waits for them, and re-layouts  6.82 us

profile of v1, /device:TPU:0, one launch (start us, length us, event | category | flops | bytes accessed | tf_op | source)
XLA Modules:
  0.0 81.7 jit_solution(9008094634931495223)
XLA Ops:
  0.0 0.0 copy-start
  0.0 1.4 %copy-done = f32[16,48,512]{2,1,0:T(8,128)S(1)} copy-done((f32[16,48,512]{2,1,0:T(8,128)S(1)}, f32[16,48,512]{2,1,0:T(8,128)}, u32[]{:S(2)}) %copy-start) | copy-done | bytes 1572888
  1.4 0.0 copy-start.1
  1.4 1.4 %copy-done.1 = f32[16,48,512]{2,1,0:T(8,128)S(1)} copy-done((f32[16,48,512]{2,1,0:T(8,128)S(1)}, f32[16,48,512]{2,1,0:T(8,128)}, u32[]{:S(2)}) %copy-start.1) | copy-done | bytes 1572888
  2.8 0.0 copy-start.2
  2.8 1.2 %copy-done.2 = f32[512,512]{1,0:T(8,128)S(1)} copy-done((f32[512,512]{1,0:T(8,128)S(1)}, f32[512,512]{1,0:T(8,128)}, u32[]{:S(2)}) %copy-start.2) | copy-done | bytes 1048600
  4.0 0.0 copy-start.3
  4.0 0.8 %copy-done.3 = f32[128,128]{1,0:T(8,128)S(1)} copy-done((f32[128,128]{1,0:T(8,128)S(1)}, f32[128,128]{1,0:T(8,128)}, u32[]{:S(2)}) %copy-start.3) | copy-done | bytes 65560
  4.9 0.0 copy-start.4
  4.9 0.8 copy-done.4
  5.7 74.9 %shard_map.55 = f32[16,48,512]{2,1,0:T(8,128)S(1)} custom-call(f32[16,48,512]{2,1,0:T(8,128)S(1)} %copy-done, f32[48,144]{1,0:T(8,128)S(1)} %copy-done.4, f32[128,128]{1,0:T(8,128)S(1)} %copy-done.3, f32[512,512]{1,0:T(8,128)S(1)} %copy-done.2, f32[16,48,512]{2,1,0:T(8,128)S(1)} %copy-done.1), custom_call_target="tpu_custom_call" | custom-call | tf_op jit(solution)/shard_map/pallas_call | solution.py:278
  80.6 1.1 %copy.7 = f32[16,48,512]{2,1,0:T(8,128)} copy(f32[16,48,512]{2,1,0:T(8,128)S(1)} %shard_map.55) | data formatting | bytes 3145728
Async XLA Ops:
  0.0 1.4 %copy-start = (f32[16,48,512]{2,1,0:T(8,128)S(1)}, f32[16,48,512]{2,1,0:T(8,128)}, u32[]{:S(2)}) copy-start(f32[16,48,512]{2,1,0:T(8,128)} %field.1) | copy-start | bytes 4718596
  1.4 1.4 %copy-start.1 = (f32[16,48,512]{2,1,0:T(8,128)S(1)}, f32[16,48,512]{2,1,0:T(8,128)}, u32[]{:S(2)}) copy-start(f32[16,48,512]{2,1,0:T(8,128)} %scaling.1) | copy-start | bytes 4718596
  2.8 1.2 %copy-start.2 = (f32[512,512]{1,0:T(8,128)S(1)}, f32[512,512]{1,0:T(8,128)}, u32[]{:S(2)}) copy-start(f32[512,512]{1,0:T(8,128)} %z_factor.1) | copy-start | bytes 3145732
  4.0 0.8 %copy-start.3 = (f32[128,128]{1,0:T(8,128)S(1)}, f32[128,128]{1,0:T(8,128)}, u32[]{:S(2)}) copy-start(f32[128,128]{1,0:T(8,128)} %y_factor.1) | copy-start | bytes 196612
  4.9 0.8 copy-start.4

commit v2 on v1

--- a/solution.py
+++ b/solution.py
@@ -9,6 +9,7 @@
 
 LANES = 128
 SUB = 16
+FETCHES = 4
 MESH = pl.DeviceIdType.MESH
 F32 = jnp.float32
 BF16 = jnp.bfloat16
@@ -77,16 +78,30 @@
 
 
 def kernel(
-    n_grp, n_blk, field, panel, y_factor, z_factor, scaling, out,
+    n_grp, n_blk, field_in, panel_in, y_in, z_in, scaling_in, out,
+    field, panel, y_factor, z_factor, scaling,
     field_high, field_low, own, partner, other, turned, gathered, mixed, back,
-    f_send, f_recv, b_send, b_recv, h1_send, h1_recv, h2_send, h2_recv,
+    in_sem, f_send, f_recv, b_send, b_recv, h1_send, h1_recv, h2_send, h2_recv,
 ):
     rows, planes, cells = field.shape
+    step_rows = rows // FETCHES
+    row_parts = [pl.ds(i * step_rows, step_rows) for i in range(FETCHES)]
+    heads = [pl.ds(0, LANES), pl.ds(LANES, cells - LANES)][: 1 + (cells > LANES)]
+    sources = [(z_in.at[heads[0]], z_factor.at[heads[0]])]
+    sources += [(field_in.at[at], field.at[at]) for at in row_parts]
+    sources += [(z_in.at[at], z_factor.at[at]) for at in heads[1:]]
+    sources += [(y_in, y_factor), (panel_in, panel), (scaling_in, scaling)]
+    fetches = [pltpu.make_async_copy(*pair, in_sem.at[i]) for i, pair in enumerate(sources)]
+    for fetch in fetches:
+        fetch.start()
     chunks = cells // LANES
     share = planes // n_grp
     piece = share * rows
     parts = h1_send.shape[1]
     part_rows = rows // parts
+    subs = f_send.shape[1]
+    sub = share // subs
+    sub_piece = sub * rows
     grp = lax.axis_index("grp")
     blk = lax.axis_index("blk")
     even = lax.rem(blk, 2) == 0
@@ -106,57 +121,79 @@
     def depth(chunk):
         z_both, z_high = stacked(z_factor[chunk * LANES:(chunk + 1) * LANES, :])
         turn = (((1,), (1,)), ((), ()))
-        for y in range(0, rows, part_rows // 2):
-            y_end = y + part_rows // 2
+        for y in range(0, rows, step_rows):
+            y_end = y + step_rows
             here = slice(y * planes, y_end * planes)
+            if chunk == 0:
+                fetches[1 + y // step_rows].wait()
+                flat = field[y:y_end].reshape(step_rows * planes, cells)
+                field_high[here, :], field_low[here, :] = split(flat)
             first = lax.dot_general(field_high[here, :], z_both, turn, preferred_element_type=F32)
             second = lax.dot_general(field_low[here, :], z_high, turn, preferred_element_type=F32)
             result = first[:, :LANES] + (first[:, LANES:] + second)
-            own[chunk, y:y_end] = result.reshape(y_end - y, planes, LANES)
+            result = result.reshape(step_rows, planes, LANES)
+            if chunk == 0:
+                for k in range(step_rows):
+                    store_turned(chunk, y + k, result[k])
+            else:
+                own[chunk, y:y_end] = result
 
     def rows_of(y):
         return pl.ds(y, planes, stride=rows)
 
+    def spot(device, at):
+        return pl.ds(pl.multiple_of(device * piece + at * sub_piece, SUB), sub_piece)
+
     def scatter(chunk):
-        for step in offsets:
-            to = lax.rem(grp + step, n_grp)
-            pltpu.make_async_remote_copy(
-                src_ref=turned.at[chunk, pl.ds(pl.multiple_of(to * piece, SUB), piece)],
-                dst_ref=gathered.at[chunk, grp],
-                send_sem=f_send.at[chunk],
-                recv_sem=f_recv.at[chunk],
-                device_id={"grp": to},
-                device_id_type=MESH,
-            ).start()
-        gathered[chunk, grp] = turned[chunk, pl.ds(pl.multiple_of(grp * piece, SUB), piece), :]
+        for at in range(subs):
+            within = pl.ds(at * sub_piece, sub_piece)
+            for step in offsets:
+                to = lax.rem(grp + step, n_grp)
+                pltpu.make_async_remote_copy(
+                    src_ref=turned.at[chunk, spot(to, at)],
+                    dst_ref=gathered.at[chunk, grp, within],
+                    send_sem=f_send.at[chunk, at],
+                    recv_sem=f_recv.at[chunk, at],
+                    device_id={"grp": to},
+                    device_id_type=MESH,
+                ).start()
+        mine = pl.ds(pl.multiple_of(grp * piece, SUB), piece)
+        gathered[chunk, grp] = turned[chunk, mine, :]
 
     def wait_for(ref, sem):
         pltpu.make_async_copy(ref, ref, sem).wait()
 
+    def incoming(chunk):
+        return gathered.at[chunk, pl.ds(0, n_grp - 1), pl.ds(0, sub_piece)]
+
     def across(chunk):
-        wait_for(gathered.at[chunk, pl.ds(0, n_grp - 1)], f_recv.at[chunk])
         y_both, y_high = stacked(y_factor[...])
-        for at in range(share):
-            pencils = jnp.concatenate(
-                [gathered[chunk, g, at * rows:(at + 1) * rows, :] for g in range(n_grp)], axis=0
-            )
-            result = times(y_both, y_high, pencils)
-            for g in range(n_grp):
-                mixed[chunk, g, at * rows:(at + 1) * rows, :] = result[g * rows:(g + 1) * rows]
-        for step in offsets:
-            to = lax.rem(grp + step, n_grp)
-            pltpu.make_async_remote_copy(
-                src_ref=mixed.at[chunk, to],
-                dst_ref=back.at[chunk, pl.ds(pl.multiple_of(grp * piece, SUB), piece)],
-                send_sem=b_send.at[chunk],
-                recv_sem=b_recv.at[chunk],
-                device_id={"grp": to},
-                device_id_type=MESH,
-            ).start()
-        back[chunk, pl.ds(pl.multiple_of(grp * piece, SUB), piece), :] = mixed[chunk, grp]
+        for at in range(subs):
+            wait_for(incoming(chunk), f_recv.at[chunk, at])
+            for plane in range(at * sub, (at + 1) * sub):
+                here = slice(plane * rows, (plane + 1) * rows)
+                pencils = jnp.concatenate(
+                    [gathered[chunk, g, here, :] for g in range(n_grp)], axis=0
+                )
+                result = times(y_both, y_high, pencils)
+                for g in range(n_grp):
+                    mixed[chunk, g, here, :] = result[g * rows:(g + 1) * rows]
+            within = pl.ds(at * sub_piece, sub_piece)
+            for step in offsets:
+                to = lax.rem(grp + step, n_grp)
+                pltpu.make_async_remote_copy(
+                    src_ref=mixed.at[chunk, to, within],
+                    dst_ref=back.at[chunk, spot(grp, at)],
+                    send_sem=b_send.at[chunk, at],
+                    recv_sem=b_recv.at[chunk, at],
+                    device_id={"grp": to},
+                    device_id_type=MESH,
+                ).start()
+            back[chunk, spot(grp, at), :] = mixed[chunk, grp, at * sub_piece:(at + 1) * sub_piece, :]
 
     def wait_back(chunk):
-        wait_for(back.at[chunk, pl.ds(0, (n_grp - 1) * piece)], b_recv.at[chunk])
+        for at in range(subs):
+            wait_for(back.at[chunk, pl.ds(0, (n_grp - 1) * sub_piece)], b_recv.at[chunk, at])
 
     def part(chunk, at):
         return (chunk, pl.ds(at * part_rows, part_rows))
@@ -213,13 +250,12 @@
         lanes = slice(chunk * LANES, (chunk + 1) * LANES)
         out[y, :, lanes] = value * scaling[y, :, lanes]
 
-    flat = field[...].reshape(rows * planes, cells)
-    field_high[...], field_low[...] = split(flat)
+    fetches[0].wait()
     depth(0)
-    for y in range(rows):
-        store_turned(0, y, own[0, y])
     pl.semaphore_wait(barrier, len(offsets) + 2)
     scatter(0)
+    for fetch in fetches[1 + FETCHES:]:
+        fetch.wait()
     for chunk in range(1, chunks):
         depth(chunk)
         for at in range(parts):
@@ -258,8 +294,9 @@
         for y in range(rows):
             store_out(chunk, y, back[chunk, rows_of(y), :])
     for chunk in range(chunks):
-        wait_for(gathered.at[chunk, pl.ds(0, n_grp - 1)], f_send.at[chunk])
-        wait_for(gathered.at[chunk, pl.ds(0, n_grp - 1)], b_send.at[chunk])
+        for at in range(subs):
+            wait_for(incoming(chunk), f_send.at[chunk, at])
+            wait_for(incoming(chunk), b_send.at[chunk, at])
         for at in range(parts):
             swap(chunk, at).wait_send()
             forward(chunk, at).wait_send()
@@ -269,21 +306,26 @@
     n_grp, n_blk = lax.axis_size("grp"), lax.axis_size("blk")
     rows, planes, cells = field.shape
     chunks = cells // LANES
-    piece = planes // n_grp * rows
+    share = planes // n_grp
+    piece = share * rows
     parts = 2
-    whole = pl.BlockSpec(memory_space=pltpu.VMEM)
+    subs = 2 if share % 2 == 0 else 1
     held = pltpu.VMEM((chunks, rows, planes, LANES), F32)
     turned = pltpu.VMEM((chunks, planes * rows, LANES), F32)
     pieces = pltpu.VMEM((chunks, n_grp, piece, LANES), F32)
     return pl.pallas_call(
         functools.partial(kernel, n_grp, n_blk),
         out_shape=jax.ShapeDtypeStruct(field.shape, F32),
-        in_specs=[whole] * 5,
-        out_specs=whole,
-        scratch_shapes=[pltpu.VMEM((rows * planes, cells), BF16)] * 2
+        in_specs=[pl.BlockSpec(memory_space=pltpu.HBM)] * 5,
+        out_specs=pl.BlockSpec(memory_space=pltpu.VMEM),
+        scratch_shapes=[
+            pltpu.VMEM(array.shape, F32) for array in (field, x_panel, y_factor, z_factor, scaling)
+        ]
+        + [pltpu.VMEM((rows * planes, cells), BF16)] * 2
         + [held] * 3
         + [turned, pieces, pieces, turned]
-        + [pltpu.SemaphoreType.DMA((chunks,))] * 4
+        + [pltpu.SemaphoreType.DMA((5 + FETCHES,))]
+        + [pltpu.SemaphoreType.DMA((chunks, subs))] * 4
         + [pltpu.SemaphoreType.DMA((chunks, parts))] * 4,
         compiler_params=pltpu.CompilerParams(
             collective_id=0, has_side_effects=True, vmem_limit_bytes=48 * 2**20

time: 82.5 us -> 85.2 us (1.033)
  Pallas kernels: 74.9 us -> 78.1 us
    pallas_call x1, Pallas kernels: 74.9 us -> 78.1 us  [fused(): pl.pallas_call(functools.partial(kernel, n_grp, n_blk), out_shape=jax.Sha...]
where the time goes in v2:
time: 85.2 us; the launch traced here: 84.9 us
  Pallas kernels  78.1 us (92%)
  local copies, waits for them, and re-layouts  6.82 us (8%)
    pallas_call x1, Pallas kernels, fused(): pl.pallas_call(functools.partial(kernel, n_grp, n_blk), out_shape=jax.Sha...  78.1 us
    unnamed x11, local copies, waits for them, and re-layouts  6.82 us

profile of v2, /device:TPU:0, one launch (start us, length us, event | category | flops | bytes accessed | tf_op | source)
XLA Modules:
  0.0 84.9 jit_solution(289647335074024650)
XLA Ops:
  0.0 0.0 copy-start
  0.0 1.4 %copy-done = f32[16,48,512]{2,1,0:T(8,128)S(1)} copy-done((f32[16,48,512]{2,1,0:T(8,128)S(1)}, f32[16,48,512]{2,1,0:T(8,128)}, u32[]{:S(2)}) %copy-start) | copy-done | bytes 1572888
  1.4 0.0 copy-start.1
  1.4 1.4 %copy-done.1 = f32[16,48,512]{2,1,0:T(8,128)S(1)} copy-done((f32[16,48,512]{2,1,0:T(8,128)S(1)}, f32[16,48,512]{2,1,0:T(8,128)}, u32[]{:S(2)}) %copy-start.1) | copy-done | bytes 1572888
  2.8 0.0 copy-start.2
  2.8 1.2 %copy-done.2 = f32[512,512]{1,0:T(8,128)S(1)} copy-done((f32[512,512]{1,0:T(8,128)S(1)}, f32[512,512]{1,0:T(8,128)}, u32[]{:S(2)}) %copy-start.2) | copy-done | bytes 1048600
  4.0 0.0 copy-start.3
  4.0 0.8 copy-done.3
  4.9 0.0 copy-start.4
  4.9 0.8 copy-done.4
  5.7 78.1 %shard_map.55 = f32[16,48,512]{2,1,0:T(8,128)S(1)} custom-call(f32[16,48,512]{2,1,0:T(8,128)S(1)} %copy-done, f32[48,144]{1,0:T(8,128)S(1)} %copy-done.4, f32[128,128]{1,0:T(8,128)S(1)} %copy-done.3, f32[512,512]{1,0:T(8,128)S(1)} %copy-done.2, f32[16,48,512]{2,1,0:T(8,128)S(1)} %copy-done.1), custom_call_target="tpu_custom_call" | custom-call | tf_op jit(solution)/shard_map/pallas_call | solution.py:316
  83.8 1.1 %copy.7 = f32[16,48,512]{2,1,0:T(8,128)} copy(f32[16,48,512]{2,1,0:T(8,128)S(1)} %shard_map.55) | data formatting | bytes 3145728
Async XLA Ops:
  0.0 1.4 %copy-start = (f32[16,48,512]{2,1,0:T(8,128)S(1)}, f32[16,48,512]{2,1,0:T(8,128)}, u32[]{:S(2)}) copy-start(f32[16,48,512]{2,1,0:T(8,128)} %field_in.1) | copy-start | bytes 4718596
  1.4 1.4 %copy-start.1 = (f32[16,48,512]{2,1,0:T(8,128)S(1)}, f32[16,48,512]{2,1,0:T(8,128)}, u32[]{:S(2)}) copy-start(f32[16,48,512]{2,1,0:T(8,128)} %scaling_in.1) | copy-start | bytes 4718596
  2.8 1.2 %copy-start.2 = (f32[512,512]{1,0:T(8,128)S(1)}, f32[512,512]{1,0:T(8,128)}, u32[]{:S(2)}) copy-start(f32[512,512]{1,0:T(8,128)} %z_in.1) | copy-start | bytes 3145732
  4.0 0.8 copy-start.3
  4.9 0.8 copy-start.4

commit v3 on v2

--- a/solution.py
+++ b/solution.py
@@ -79,9 +79,9 @@
 
 def kernel(
     n_grp, n_blk, field_in, panel_in, y_in, z_in, scaling_in, out,
-    field, panel, y_factor, z_factor, scaling,
+    field, panel, y_factor, z_factor, scaling, done,
     field_high, field_low, own, partner, other, turned, gathered, mixed, back,
-    in_sem, f_send, f_recv, b_send, b_recv, h1_send, h1_recv, h2_send, h2_recv,
+    in_sem, out_sem, f_send, f_recv, b_send, b_recv, h1_send, h1_recv, h2_send, h2_recv,
 ):
     rows, planes, cells = field.shape
     step_rows = rows // FETCHES
@@ -246,9 +246,17 @@
     def store_turned(chunk, y, value):
         turned[chunk, rows_of(y), :] = value
 
+    def written(chunk, at):
+        return pltpu.make_async_copy(
+            done.at[chunk, row_parts[at]],
+            out.at[row_parts[at], :, pl.ds(chunk * LANES, LANES)],
+            out_sem.at[chunk, at],
+        )
+
     def store_out(chunk, y, value):
-        lanes = slice(chunk * LANES, (chunk + 1) * LANES)
-        out[y, :, lanes] = value * scaling[y, :, lanes]
+        done[chunk, y] = value * scaling[y, :, chunk * LANES:(chunk + 1) * LANES]
+        if (y + 1) % step_rows == 0:
+            written(chunk, y // step_rows).start()
 
     fetches[0].wait()
     depth(0)
@@ -294,6 +302,8 @@
         for y in range(rows):
             store_out(chunk, y, back[chunk, rows_of(y), :])
     for chunk in range(chunks):
+        for at in range(FETCHES):
+            written(chunk, at).wait()
         for at in range(subs):
             wait_for(incoming(chunk), f_send.at[chunk, at])
             wait_for(incoming(chunk), b_send.at[chunk, at])
@@ -308,7 +318,7 @@
     chunks = cells // LANES
     share = planes // n_grp
     piece = share * rows
-    parts = 2
+    parts = 4
     subs = 2 if share % 2 == 0 else 1
     held = pltpu.VMEM((chunks, rows, planes, LANES), F32)
     turned = pltpu.VMEM((chunks, planes * rows, LANES), F32)
@@ -317,18 +327,20 @@
         functools.partial(kernel, n_grp, n_blk),
         out_shape=jax.ShapeDtypeStruct(field.shape, F32),
         in_specs=[pl.BlockSpec(memory_space=pltpu.HBM)] * 5,
-        out_specs=pl.BlockSpec(memory_space=pltpu.VMEM),
+        out_specs=pl.BlockSpec(memory_space=pltpu.HBM),
         scratch_shapes=[
             pltpu.VMEM(array.shape, F32) for array in (field, x_panel, y_factor, z_factor, scaling)
         ]
+        + [held]
         + [pltpu.VMEM((rows * planes, cells), BF16)] * 2
         + [held] * 3
         + [turned, pieces, pieces, turned]
         + [pltpu.SemaphoreType.DMA((5 + FETCHES,))]
+        + [pltpu.SemaphoreType.DMA((chunks, FETCHES))]
         + [pltpu.SemaphoreType.DMA((chunks, subs))] * 4
         + [pltpu.SemaphoreType.DMA((chunks, parts))] * 4,
         compiler_params=pltpu.CompilerParams(
-            collective_id=0, has_side_effects=True, vmem_limit_bytes=48 * 2**20
+            collective_id=0, has_side_effects=True, vmem_limit_bytes=60 * 2**20
         ),
     )(field, x_panel, y_factor, z_factor, scaling)
 

time: 85.2 us -> 81.1 us (0.952)
  local copies, waits for them, and re-layouts: 6.82 us -> 2.71 us
    unnamed x11 -> x1, local copies, waits for them, and re-layouts: 6.82 us -> 2.71 us
where the time goes in v3:
time: 81.1 us; the launch traced here: 81 us
  Pallas kernels  78.3 us (97%)
  local copies, waits for them, and re-layouts  2.71 us (3%)
    pallas_call x1, Pallas kernels, fused(): pl.pallas_call(functools.partial(kernel, n_grp, n_blk), out_shape=jax.Sha...  78.3 us
    unnamed x1, local copies, waits for them, and re-layouts  2.71 us

profile of v3, /device:TPU:0, one launch (start us, length us, event | category | flops | bytes accessed | tf_op | source)
XLA Modules:
  0.0 81.0 jit_solution(6679246310378426955)
XLA Ops:
  0.0 78.3 %shard_map.55 = f32[16,48,512]{2,1,0:T(8,128)} custom-call(f32[16,48,512]{2,1,0:T(8,128)} %field_in.1, f32[48,144]{1,0:T(8,128)} %panel_in.1, f32[128,128]{1,0:T(8,128)} %y_in.1, f32[512,512]{1,0:T(8,128)} %z_in.1, f32[16,48,512]{2,1,0:T(8,128)} %scaling_in.1), custom_call_target="tpu_custom_call" | custom-call | tf_op jit(solution)/shard_map/pallas_call | solution.py:326
  78.3 2.7 %copy.7 = f32[16,48,512]{2,1,0:T(8,128)} copy(f32[16,48,512]{2,1,0:T(8,128)} %shard_map.55) | data formatting | bytes 3145728

commit v4 on v3

--- a/solution.py
+++ b/solution.py
@@ -86,9 +86,18 @@
     rows, planes, cells = field.shape
     step_rows = rows // FETCHES
     row_parts = [pl.ds(i * step_rows, step_rows) for i in range(FETCHES)]
+    grp = lax.axis_index("grp")
+    blk = lax.axis_index("blk")
+    half_grp, half_planes = n_grp // 2, planes // 2
+    far = jnp.where(grp < half_grp, 1, 0)
+    near = 1 - far
+    starts = [pl.multiple_of(half * half_planes, SUB // 2) for half in (far, near)]
     heads = [pl.ds(0, LANES), pl.ds(LANES, cells - LANES)][: 1 + (cells > LANES)]
     sources = [(z_in.at[heads[0]], z_factor.at[heads[0]])]
-    sources += [(field_in.at[at], field.at[at]) for at in row_parts]
+    for start in starts:
+        for at in row_parts:
+            place = (at, pl.ds(start, half_planes))
+            sources.append((field_in.at[place], field.at[place]))
     sources += [(z_in.at[at], z_factor.at[at]) for at in heads[1:]]
     sources += [(y_in, y_factor), (panel_in, panel), (scaling_in, scaling)]
     fetches = [pltpu.make_async_copy(*pair, in_sem.at[i]) for i, pair in enumerate(sources)]
@@ -102,41 +111,49 @@
     subs = f_send.shape[1]
     sub = share // subs
     sub_piece = sub * rows
-    grp = lax.axis_index("grp")
-    blk = lax.axis_index("blk")
     even = lax.rem(blk, 2) == 0
     mate = jnp.where(even, blk + 1, blk - 1)
     ahead = lax.rem(jnp.where(even, blk + 2, blk + n_blk - 2), n_blk)
     behind = lax.rem(jnp.where(even, blk + n_blk - 2, blk + 2), n_blk)
 
-    offsets = sorted(range(1, n_grp), key=lambda s: (-min(s, n_grp - s), s))
+    far_ids = [far * half_grp + lax.rem(grp + k, half_grp) for k in range(half_grp)]
+    near_ids = [near * half_grp + lax.rem(grp + k, half_grp) for k in range(1, half_grp)]
     barrier = pltpu.get_barrier_semaphore()
-    for step in offsets:
-        pl.semaphore_signal(
-            barrier, inc=1, device_id={"grp": lax.rem(grp + step, n_grp)}, device_id_type=MESH
-        )
+    for to in far_ids + near_ids:
+        pl.semaphore_signal(barrier, inc=1, device_id={"grp": to}, device_id_type=MESH)
     pl.semaphore_signal(barrier, inc=1, device_id={"blk": mate}, device_id_type=MESH)
     pl.semaphore_signal(barrier, inc=1, device_id={"blk": behind}, device_id_type=MESH)
 
+    def times_z(high, low, z_both, z_high):
+        turn = (((1,), (1,)), ((), ()))
+        first = lax.dot_general(high, z_both, turn, preferred_element_type=F32)
+        second = lax.dot_general(low, z_high, turn, preferred_element_type=F32)
+        return first[:, :LANES] + (first[:, LANES:] + second)
+
+    def z_rows(chunk):
+        return stacked(z_factor[chunk * LANES:(chunk + 1) * LANES, :])
+
+    def first_depth(which, z_both, z_high):
+        start = starts[which]
+        for at in range(FETCHES):
+            fetches[1 + which * FETCHES + at].wait()
+            y = at * step_rows
+            block = field[y:y + step_rows, pl.ds(start, half_planes), :]
+            high, low = split(block.reshape(step_rows * half_planes, cells))
+            result = times_z(high, low, z_both, z_high).reshape(step_rows, half_planes, LANES)
+            for k in range(step_rows):
+                turned[0, pl.ds(start * rows + y + k, half_planes, stride=rows), :] = result[k]
+
     def depth(chunk):
-        z_both, z_high = stacked(z_factor[chunk * LANES:(chunk + 1) * LANES, :])
-        turn = (((1,), (1,)), ((), ()))
+        z_both, z_high = z_rows(chunk)
         for y in range(0, rows, step_rows):
             y_end = y + step_rows
             here = slice(y * planes, y_end * planes)
-            if chunk == 0:
-                fetches[1 + y // step_rows].wait()
+            if chunk == 1:
                 flat = field[y:y_end].reshape(step_rows * planes, cells)
                 field_high[here, :], field_low[here, :] = split(flat)
-            first = lax.dot_general(field_high[here, :], z_both, turn, preferred_element_type=F32)
-            second = lax.dot_general(field_low[here, :], z_high, turn, preferred_element_type=F32)
-            result = first[:, :LANES] + (first[:, LANES:] + second)
-            result = result.reshape(step_rows, planes, LANES)
-            if chunk == 0:
-                for k in range(step_rows):
-                    store_turned(chunk, y + k, result[k])
-            else:
-                own[chunk, y:y_end] = result
+            result = times_z(field_high[here, :], field_low[here, :], z_both, z_high)
+            own[chunk, y:y_end] = result.reshape(step_rows, planes, LANES)
 
     def rows_of(y):
         return pl.ds(y, planes, stride=rows)
@@ -144,11 +161,10 @@
     def spot(device, at):
         return pl.ds(pl.multiple_of(device * piece + at * sub_piece, SUB), sub_piece)
 
-    def scatter(chunk):
+    def scatter(chunk, ids):
         for at in range(subs):
             within = pl.ds(at * sub_piece, sub_piece)
-            for step in offsets:
-                to = lax.rem(grp + step, n_grp)
+            for to in ids:
                 pltpu.make_async_remote_copy(
                     src_ref=turned.at[chunk, spot(to, at)],
                     dst_ref=gathered.at[chunk, grp, within],
@@ -157,6 +173,8 @@
                     device_id={"grp": to},
                     device_id_type=MESH,
                 ).start()
+
+    def keep(chunk):
         mine = pl.ds(pl.multiple_of(grp * piece, SUB), piece)
         gathered[chunk, grp] = turned[chunk, mine, :]
 
@@ -179,8 +197,7 @@
                 for g in range(n_grp):
                     mixed[chunk, g, here, :] = result[g * rows:(g + 1) * rows]
             within = pl.ds(at * sub_piece, sub_piece)
-            for step in offsets:
-                to = lax.rem(grp + step, n_grp)
+            for to in far_ids + near_ids:
                 pltpu.make_async_remote_copy(
                     src_ref=mixed.at[chunk, to, within],
                     dst_ref=back.at[chunk, spot(grp, at)],
@@ -259,10 +276,14 @@
             written(chunk, y // step_rows).start()
 
     fetches[0].wait()
-    depth(0)
-    pl.semaphore_wait(barrier, len(offsets) + 2)
-    scatter(0)
-    for fetch in fetches[1 + FETCHES:]:
+    z_both, z_high = z_rows(0)
+    first_depth(0, z_both, z_high)
+    pl.semaphore_wait(barrier, n_grp + 1)
+    scatter(0, far_ids)
+    first_depth(1, z_both, z_high)
+    scatter(0, near_ids)
+    keep(0)
+    for fetch in fetches[1 + 2 * FETCHES:]:
         fetch.wait()
     for chunk in range(1, chunks):
         depth(chunk)
@@ -285,7 +306,8 @@
         else:
             across(chunk - 2)
         along(chunk, store_turned)
-        scatter(chunk)
+        scatter(chunk, far_ids + near_ids)
+        keep(chunk)
     if chunks < 2:
         across(0)
     if chunks < 3:
@@ -312,6 +334,15 @@
             forward(chunk, at).wait_send()
 
 
+def hand_on(source, target, sem):
+    rows = source.shape[0]
+    copies = [pltpu.make_async_copy(source.at[i], target.at[i], sem.at[i]) for i in range(rows)]
+    for copy in copies:
+        copy.start()
+    for copy in copies:
+        copy.wait()
+
+
 def fused(field, x_panel, y_factor, z_factor, scaling):
     n_grp, n_blk = lax.axis_size("grp"), lax.axis_size("blk")
     rows, planes, cells = field.shape
@@ -323,7 +354,7 @@
     held = pltpu.VMEM((chunks, rows, planes, LANES), F32)
     turned = pltpu.VMEM((chunks, planes * rows, LANES), F32)
     pieces = pltpu.VMEM((chunks, n_grp, piece, LANES), F32)
-    return pl.pallas_call(
+    result = pl.pallas_call(
         functools.partial(kernel, n_grp, n_blk),
         out_shape=jax.ShapeDtypeStruct(field.shape, F32),
         in_specs=[pl.BlockSpec(memory_space=pltpu.HBM)] * 5,
@@ -335,7 +366,7 @@
         + [pltpu.VMEM((rows * planes, cells), BF16)] * 2
         + [held] * 3
         + [turned, pieces, pieces, turned]
-        + [pltpu.SemaphoreType.DMA((5 + FETCHES,))]
+        + [pltpu.SemaphoreType.DMA((5 + 2 * FETCHES,))]
         + [pltpu.SemaphoreType.DMA((chunks, FETCHES))]
         + [pltpu.SemaphoreType.DMA((chunks, subs))] * 4
         + [pltpu.SemaphoreType.DMA((chunks, parts))] * 4,
@@ -343,6 +374,14 @@
             collective_id=0, has_side_effects=True, vmem_limit_bytes=60 * 2**20
         ),
     )(field, x_panel, y_factor, z_factor, scaling)
+    return pl.pallas_call(
+        hand_on,
+        out_shape=jax.ShapeDtypeStruct(field.shape, F32),
+        in_specs=[pl.BlockSpec(memory_space=pltpu.HBM)],
+        out_specs=pl.BlockSpec(memory_space=pltpu.HBM),
+        scratch_shapes=[pltpu.SemaphoreType.DMA((rows,))],
+        compiler_params=pltpu.CompilerParams(vmem_limit_bytes=60 * 2**20),
+    )(result)
 
 
 def on_device(field, x_panel, y_factor, z_factor, scaling):
@@ -352,7 +391,7 @@
         x_panel.shape[1] == 3 * planes
         and n_blk >= 4
         and n_blk % 2 == 0
-        and n_grp >= 2
+        and n_grp % 2 == 0
         and planes % n_grp == 0
         and planes % SUB == 0
         and rows % SUB == 0

time: 81.1 us -> 128 us (1.58)
  Pallas kernels: 78.3 us -> 128 us
  local copies, waits for them, and re-layouts: 2.71 us -> 0 us
    pallas_call x0 -> x1, Pallas kernels: none -> 48.9 us  [fused(): pl.pallas_call(hand_on, out_shape=jax.ShapeDtypeStruct(field.shape, F32),...]
    unnamed x1 -> x0, local copies, waits for them, and re-layouts: 2.71 us -> none
where the time goes in v4:
time: 128 us
  Pallas kernels  128 us (100%)
    pallas_call x1, Pallas kernels, fused(): pl.pallas_call(functools.partial(kernel, n_grp, n_blk), out_shape=jax.Sha...  79.2 us
    pallas_call x1, Pallas kernels, fused(): pl.pallas_call(hand_on, out_shape=jax.ShapeDtypeStruct(field.shape, F32),...  48.9 us

profile of v4, /device:TPU:0, one launch (start us, length us, event | category | flops | bytes accessed | tf_op | source)
XLA Modules:
  0.0 128.1 jit_solution(15883551924089726579)
XLA Ops:
  0.0 79.2 %shard_map.55.source = f32[16,48,512]{2,1,0:T(8,128)} custom-call(f32[16,48,512]{2,1,0:T(8,128)} %field_in.1, f32[48,144]{1,0:T(8,128)} %panel_in.1, f32[128,128]{1,0:T(8,128)} %y_in.1, f32[512,512]{1,0:T(8,128)} %z_in.1, f32[16,48,512]{2,1,0:T(8,128)} %scaling_in.1), custom_call_target="tpu_custom_call" | custom-call | tf_op jit(solution)/shard_map/pallas_call | solution.py:357
  79.2 48.9 %shard_map.56 = f32[16,48,512]{2,1,0:T(8,128)} custom-call(f32[16,48,512]{2,1,0:T(8,128)} %shard_map.55.source), custom_call_target="tpu_custom_call" | custom-call | tf_op jit(solution)/shard_map/pallas_call | solution.py:377

commit v5 on v2

--- a/solution.py
+++ b/solution.py
@@ -92,7 +92,8 @@
     sources += [(z_in.at[at], z_factor.at[at]) for at in heads[1:]]
     sources += [(y_in, y_factor), (panel_in, panel), (scaling_in, scaling)]
     fetches = [pltpu.make_async_copy(*pair, in_sem.at[i]) for i, pair in enumerate(sources)]
-    for fetch in fetches:
+    now, later = fetches[: 1 + FETCHES], fetches[1 + FETCHES:]
+    for fetch in now:
         fetch.start()
     chunks = cells // LANES
     share = planes // n_grp
@@ -252,9 +253,11 @@
 
     fetches[0].wait()
     depth(0)
+    for fetch in later:
+        fetch.start()
     pl.semaphore_wait(barrier, len(offsets) + 2)
     scatter(0)
-    for fetch in fetches[1 + FETCHES:]:
+    for fetch in later:
         fetch.wait()
     for chunk in range(1, chunks):
         depth(chunk)
@@ -289,17 +292,19 @@
     along(0, store_out)
     for chunk in late[-1:]:
         across(chunk)
+    for chunk in range(chunks):
+        for at in range(parts):
+            swap(chunk, at).wait_send()
+            forward(chunk, at).wait_send()
+        for at in range(subs):
+            wait_for(incoming(chunk), f_send.at[chunk, at])
     for chunk in range(1, chunks):
         wait_back(chunk)
         for y in range(rows):
             store_out(chunk, y, back[chunk, rows_of(y), :])
     for chunk in range(chunks):
         for at in range(subs):
-            wait_for(incoming(chunk), f_send.at[chunk, at])
             wait_for(incoming(chunk), b_send.at[chunk, at])
-        for at in range(parts):
-            swap(chunk, at).wait_send()
-            forward(chunk, at).wait_send()
 
 
 def fused(field, x_panel, y_factor, z_factor, scaling):
@@ -308,14 +313,14 @@
     chunks = cells // LANES
     share = planes // n_grp
     piece = share * rows
-    parts = 2
+    parts = 4
     subs = 2 if share % 2 == 0 else 1
     held = pltpu.VMEM((chunks, rows, planes, LANES), F32)
     turned = pltpu.VMEM((chunks, planes * rows, LANES), F32)
     pieces = pltpu.VMEM((chunks, n_grp, piece, LANES), F32)
     return pl.pallas_call(
         functools.partial(kernel, n_grp, n_blk),
-        out_shape=jax.ShapeDtypeStruct(field.shape, F32),
+        out_shape=pltpu.VMEM(field.shape, F32),
         in_specs=[pl.BlockSpec(memory_space=pltpu.HBM)] * 5,
         out_specs=pl.BlockSpec(memory_space=pltpu.VMEM),
         scratch_shapes=[
@@ -328,9 +333,12 @@
         + [pltpu.SemaphoreType.DMA((chunks, subs))] * 4
         + [pltpu.SemaphoreType.DMA((chunks, parts))] * 4,
         compiler_params=pltpu.CompilerParams(
-            collective_id=0, has_side_effects=True, vmem_limit_bytes=48 * 2**20
+            collective_id=0, has_side_effects=True, vmem_limit_bytes=40 * 2**20
         ),
-    )(field, x_panel, y_factor, z_factor, scaling)
+    )(*(
+        pltpu.with_memory_space_constraint(array, pltpu.HBM)
+        for array in (field, x_panel, y_factor, z_factor, scaling)
+    ))
 
 
 def on_device(field, x_panel, y_factor, z_factor, scaling):

time: 85.2 us -> 80 us (0.939)
  local copies, waits for them, and re-layouts: 6.82 us -> 1.15 us
    unnamed x11 -> x1, local copies, waits for them, and re-layouts: 6.82 us -> 1.15 us
where the time goes in v5:
time: 80 us; the launch traced here: 79.9 us
  Pallas kernels  78.7 us (98%)
  local copies, waits for them, and re-layouts  1.15 us (1%)
    pallas_call x1, Pallas kernels, fused(): pl.pallas_call(functools.partial(kernel, n_grp, n_blk), out_shape=pltpu.V...  78.7 us

profile of v5, /device:TPU:0, one launch (start us, length us, event | category | flops | bytes accessed | tf_op | source)
XLA Modules:
  0.0 79.9 jit_solution(7120884473140799754)
XLA Ops:
  0.0 78.7 %shard_map.55 = f32[16,48,512]{2,1,0:T(8,128)S(1)} custom-call(f32[16,48,512]{2,1,0:T(8,128)} %field_in.1, f32[48,144]{1,0:T(8,128)} %panel_in.1, f32[128,128]{1,0:T(8,128)} %y_in.1, f32[512,512]{1,0:T(8,128)} %z_in.1, f32[16,48,512]{2,1,0:T(8,128)} %scaling_in.1), custom_call_target="tpu_custom_call" | custom-call | tf_op jit(solution)/shard_map/pallas_call | solution.py:321
  78.7 1.1 %copy.7 = f32[16,48,512]{2,1,0:T(8,128)} copy(f32[16,48,512]{2,1,0:T(8,128)S(1)} %shard_map.55) | data formatting | bytes 3145728

commit v6 on v4

--- a/solution.py
+++ b/solution.py
@@ -79,9 +79,9 @@
 
 def kernel(
     n_grp, n_blk, field_in, panel_in, y_in, z_in, scaling_in, out,
-    field, panel, y_factor, z_factor, scaling, done,
+    field, panel, y_factor, z_factor, scaling,
     field_high, field_low, own, partner, other, turned, gathered, mixed, back,
-    in_sem, out_sem, f_send, f_recv, b_send, b_recv, h1_send, h1_recv, h2_send, h2_recv,
+    in_sem, f_send, f_recv, b_send, b_recv, h1_send, h1_recv, h2_send, h2_recv,
 ):
     rows, planes, cells = field.shape
     step_rows = rows // FETCHES
@@ -101,7 +101,8 @@
     sources += [(z_in.at[at], z_factor.at[at]) for at in heads[1:]]
     sources += [(y_in, y_factor), (panel_in, panel), (scaling_in, scaling)]
     fetches = [pltpu.make_async_copy(*pair, in_sem.at[i]) for i, pair in enumerate(sources)]
-    for fetch in fetches:
+    now, later = fetches[: 1 + 2 * FETCHES], fetches[1 + 2 * FETCHES:]
+    for fetch in now:
         fetch.start()
     chunks = cells // LANES
     share = planes // n_grp
@@ -118,8 +119,10 @@
 
     far_ids = [far * half_grp + lax.rem(grp + k, half_grp) for k in range(half_grp)]
     near_ids = [near * half_grp + lax.rem(grp + k, half_grp) for k in range(1, half_grp)]
+    offsets = sorted(range(1, n_grp), key=lambda s: (-min(s, n_grp - s), s))
+    mixed_ids = [lax.rem(grp + step, n_grp) for step in offsets]
     barrier = pltpu.get_barrier_semaphore()
-    for to in far_ids + near_ids:
+    for to in mixed_ids:
         pl.semaphore_signal(barrier, inc=1, device_id={"grp": to}, device_id_type=MESH)
     pl.semaphore_signal(barrier, inc=1, device_id={"blk": mate}, device_id_type=MESH)
     pl.semaphore_signal(barrier, inc=1, device_id={"blk": behind}, device_id_type=MESH)
@@ -197,7 +200,7 @@
                 for g in range(n_grp):
                     mixed[chunk, g, here, :] = result[g * rows:(g + 1) * rows]
             within = pl.ds(at * sub_piece, sub_piece)
-            for to in far_ids + near_ids:
+            for to in mixed_ids:
                 pltpu.make_async_remote_copy(
                     src_ref=mixed.at[chunk, to, within],
                     dst_ref=back.at[chunk, spot(grp, at)],
@@ -263,27 +266,21 @@
     def store_turned(chunk, y, value):
         turned[chunk, rows_of(y), :] = value
 
-    def written(chunk, at):
-        return pltpu.make_async_copy(
-            done.at[chunk, row_parts[at]],
-            out.at[row_parts[at], :, pl.ds(chunk * LANES, LANES)],
-            out_sem.at[chunk, at],
-        )
-
     def store_out(chunk, y, value):
-        done[chunk, y] = value * scaling[y, :, chunk * LANES:(chunk + 1) * LANES]
-        if (y + 1) % step_rows == 0:
-            written(chunk, y // step_rows).start()
+        lanes = slice(chunk * LANES, (chunk + 1) * LANES)
+        out[y, :, lanes] = value * scaling[y, :, lanes]
 
     fetches[0].wait()
     z_both, z_high = z_rows(0)
     first_depth(0, z_both, z_high)
-    pl.semaphore_wait(barrier, n_grp + 1)
+    pl.semaphore_wait(barrier, len(offsets) + 2)
     scatter(0, far_ids)
+    for fetch in later:
+        fetch.start()
     first_depth(1, z_both, z_high)
     scatter(0, near_ids)
     keep(0)
-    for fetch in fetches[1 + 2 * FETCHES:]:
+    for fetch in later:
         fetch.wait()
     for chunk in range(1, chunks):
         depth(chunk)
@@ -306,7 +303,7 @@
         else:
             across(chunk - 2)
         along(chunk, store_turned)
-        scatter(chunk, far_ids + near_ids)
+        scatter(chunk, mixed_ids)
         keep(chunk)
     if chunks < 2:
         across(0)
@@ -319,28 +316,19 @@
     along(0, store_out)
     for chunk in late[-1:]:
         across(chunk)
+    for chunk in range(chunks):
+        for at in range(parts):
+            swap(chunk, at).wait_send()
+            forward(chunk, at).wait_send()
+        for at in range(subs):
+            wait_for(incoming(chunk), f_send.at[chunk, at])
     for chunk in range(1, chunks):
         wait_back(chunk)
         for y in range(rows):
             store_out(chunk, y, back[chunk, rows_of(y), :])
     for chunk in range(chunks):
-        for at in range(FETCHES):
-            written(chunk, at).wait()
-        for at in range(subs):
-            wait_for(incoming(chunk), f_send.at[chunk, at])
+        for at in range(subs):
             wait_for(incoming(chunk), b_send.at[chunk, at])
-        for at in range(parts):
-            swap(chunk, at).wait_send()
-            forward(chunk, at).wait_send()
-
-
-def hand_on(source, target, sem):
-    rows = source.shape[0]
-    copies = [pltpu.make_async_copy(source.at[i], target.at[i], sem.at[i]) for i in range(rows)]
-    for copy in copies:
-        copy.start()
-    for copy in copies:
-        copy.wait()
 
 
 def fused(field, x_panel, y_factor, z_factor, scaling):
@@ -354,34 +342,27 @@
     held = pltpu.VMEM((chunks, rows, planes, LANES), F32)
     turned = pltpu.VMEM((chunks, planes * rows, LANES), F32)
     pieces = pltpu.VMEM((chunks, n_grp, piece, LANES), F32)
-    result = pl.pallas_call(
+    return pl.pallas_call(
         functools.partial(kernel, n_grp, n_blk),
-        out_shape=jax.ShapeDtypeStruct(field.shape, F32),
+        out_shape=pltpu.VMEM(field.shape, F32),
         in_specs=[pl.BlockSpec(memory_space=pltpu.HBM)] * 5,
-        out_specs=pl.BlockSpec(memory_space=pltpu.HBM),
+        out_specs=pl.BlockSpec(memory_space=pltpu.VMEM),
         scratch_shapes=[
             pltpu.VMEM(array.shape, F32) for array in (field, x_panel, y_factor, z_factor, scaling)
         ]
-        + [held]
         + [pltpu.VMEM((rows * planes, cells), BF16)] * 2
         + [held] * 3
         + [turned, pieces, pieces, turned]
         + [pltpu.SemaphoreType.DMA((5 + 2 * FETCHES,))]
-        + [pltpu.SemaphoreType.DMA((chunks, FETCHES))]
         + [pltpu.SemaphoreType.DMA((chunks, subs))] * 4
         + [pltpu.SemaphoreType.DMA((chunks, parts))] * 4,
         compiler_params=pltpu.CompilerParams(
-            collective_id=0, has_side_effects=True, vmem_limit_bytes=60 * 2**20
+            collective_id=0, has_side_effects=True, vmem_limit_bytes=40 * 2**20
         ),
-    )(field, x_panel, y_factor, z_factor, scaling)
-    return pl.pallas_call(
-        hand_on,
-        out_shape=jax.ShapeDtypeStruct(field.shape, F32),
-        in_specs=[pl.BlockSpec(memory_space=pltpu.HBM)],
-        out_specs=pl.BlockSpec(memory_space=pltpu.HBM),
-        scratch_shapes=[pltpu.SemaphoreType.DMA((rows,))],
-        compiler_params=pltpu.CompilerParams(vmem_limit_bytes=60 * 2**20),
-    )(result)
+    )(*(
+        pltpu.with_memory_space_constraint(array, pltpu.HBM)
+        for array in (field, x_panel, y_factor, z_factor, scaling)
+    ))
 
 
 def on_device(field, x_panel, y_factor, z_factor, scaling):

time: 128 us -> 80.2 us (0.63)
  Pallas kernels: 128 us -> 78.9 us
    pallas_call x2 -> x1, Pallas kernels: 128 us -> 78.9 us  [fused(): pl.pallas_call(functools.partial(kernel, n_grp, n_blk), out_shape=pltpu.V...]
where the time goes in v6:
time: 80.2 us; the launch traced here: 80.1 us
  Pallas kernels  78.9 us (98%)
  local copies, waits for them, and re-layouts  1.15 us (1%)
    pallas_call x1, Pallas kernels, fused(): pl.pallas_call(functools.partial(kernel, n_grp, n_blk), out_shape=pltpu.V...  78.9 us

profile of v6, /device:TPU:0, one launch (start us, length us, event | category | flops | bytes accessed | tf_op | source)
XLA Modules:
  0.0 80.1 jit_solution(14755063913158327329)
XLA Ops:
  0.0 78.9 %shard_map.55 = f32[16,48,512]{2,1,0:T(8,128)S(1)} custom-call(f32[16,48,512]{2,1,0:T(8,128)} %field_in.1, f32[48,144]{1,0:T(8,128)} %panel_in.1, f32[128,128]{1,0:T(8,128)} %y_in.1, f32[512,512]{1,0:T(8,128)} %z_in.1, f32[16,48,512]{2,1,0:T(8,128)} %scaling_in.1), custom_call_target="tpu_custom_call" | custom-call | tf_op jit(solution)/shard_map/pallas_call | solution.py:345
  78.9 1.1 %copy.7 = f32[16,48,512]{2,1,0:T(8,128)} copy(f32[16,48,512]{2,1,0:T(8,128)S(1)} %shard_map.55) | data formatting | bytes 3145728

commit v7 on v6

--- a/solution.py
+++ b/solution.py
@@ -187,29 +187,32 @@
     def incoming(chunk):
         return gathered.at[chunk, pl.ds(0, n_grp - 1), pl.ds(0, sub_piece)]
 
+    def across_part(chunk, at):
+        y_both, y_high = stacked(y_factor[...])
+        wait_for(incoming(chunk), f_recv.at[chunk, at])
+        for plane in range(at * sub, (at + 1) * sub):
+            here = slice(plane * rows, (plane + 1) * rows)
+            pencils = jnp.concatenate(
+                [gathered[chunk, g, here, :] for g in range(n_grp)], axis=0
+            )
+            result = times(y_both, y_high, pencils)
+            for g in range(n_grp):
+                mixed[chunk, g, here, :] = result[g * rows:(g + 1) * rows]
+        within = pl.ds(at * sub_piece, sub_piece)
+        for to in mixed_ids:
+            pltpu.make_async_remote_copy(
+                src_ref=mixed.at[chunk, to, within],
+                dst_ref=back.at[chunk, spot(grp, at)],
+                send_sem=b_send.at[chunk, at],
+                recv_sem=b_recv.at[chunk, at],
+                device_id={"grp": to},
+                device_id_type=MESH,
+            ).start()
+        back[chunk, spot(grp, at), :] = mixed[chunk, grp, at * sub_piece:(at + 1) * sub_piece, :]
+
     def across(chunk):
-        y_both, y_high = stacked(y_factor[...])
         for at in range(subs):
-            wait_for(incoming(chunk), f_recv.at[chunk, at])
-            for plane in range(at * sub, (at + 1) * sub):
-                here = slice(plane * rows, (plane + 1) * rows)
-                pencils = jnp.concatenate(
-                    [gathered[chunk, g, here, :] for g in range(n_grp)], axis=0
-                )
-                result = times(y_both, y_high, pencils)
-                for g in range(n_grp):
-                    mixed[chunk, g, here, :] = result[g * rows:(g + 1) * rows]
-            within = pl.ds(at * sub_piece, sub_piece)
-            for to in mixed_ids:
-                pltpu.make_async_remote_copy(
-                    src_ref=mixed.at[chunk, to, within],
-                    dst_ref=back.at[chunk, spot(grp, at)],
-                    send_sem=b_send.at[chunk, at],
-                    recv_sem=b_recv.at[chunk, at],
-                    device_id={"grp": to},
-                    device_id_type=MESH,
-                ).start()
-            back[chunk, spot(grp, at), :] = mixed[chunk, grp, at * sub_piece:(at + 1) * sub_piece, :]
+            across_part(chunk, at)
 
     def wait_back(chunk):
         for at in range(subs):
@@ -238,10 +241,13 @@
             device_id_type=MESH,
         )
 
+    def pass_part(chunk, at):
+        swap(chunk, at).wait_recv()
+        forward(chunk, at).start()
+
     def pass_on(chunk):
         for at in range(parts):
-            swap(chunk, at).wait_recv()
-            forward(chunk, at).start()
+            pass_part(chunk, at)
 
     def along(chunk, store):
         left, mid, right = (panel[:, i * planes:(i + 1) * planes] for i in range(3))
@@ -295,12 +301,16 @@
             swap(0, at).start()
 
     for chunk in range(1, chunks):
-        pass_on(chunk)
         if chunk == 1:
-            across(0)
+            for at in range(parts):
+                pass_part(chunk, at)
+                if at % (parts // subs) == 0:
+                    across_part(0, at // (parts // subs))
         elif chunk == 2:
+            pass_on(chunk)
             first_home()
         else:
+            pass_on(chunk)
             across(chunk - 2)
         along(chunk, store_turned)
         scatter(chunk, mixed_ids)

time: 80.2 us -> 76.6 us (0.955)
  Pallas kernels: 78.9 us -> 75.3 us
    pallas_call x1, Pallas kernels: 78.9 us -> 75.3 us  [fused(): pl.pallas_call(functools.partial(kernel, n_grp, n_blk), out_shape=pltpu.V...]
where the time goes in v7:
time: 76.6 us; the launch traced here: 76.4 us
  Pallas kernels  75.3 us (98%)
  local copies, waits for them, and re-layouts  1.15 us (2%)
    pallas_call x1, Pallas kernels, fused(): pl.pallas_call(functools.partial(kernel, n_grp, n_blk), out_shape=pltpu.V...  75.3 us

profile of v7, /device:TPU:0, one launch (start us, length us, event | category | flops | bytes accessed | tf_op | source)
XLA Modules:
  0.0 76.4 jit_solution(13470573045255850137)
XLA Ops:
  0.0 75.3 %shard_map.55 = f32[16,48,512]{2,1,0:T(8,128)S(1)} custom-call(f32[16,48,512]{2,1,0:T(8,128)} %field_in.1, f32[48,144]{1,0:T(8,128)} %panel_in.1, f32[128,128]{1,0:T(8,128)} %y_in.1, f32[512,512]{1,0:T(8,128)} %z_in.1, f32[16,48,512]{2,1,0:T(8,128)} %scaling_in.1), custom_call_target="tpu_custom_call" | custom-call | tf_op jit(solution)/shard_map/pallas_call | solution.py:355
  75.3 1.1 %copy.7 = f32[16,48,512]{2,1,0:T(8,128)} copy(f32[16,48,512]{2,1,0:T(8,128)S(1)} %shard_map.55) | data formatting | bytes 3145728
